TPU v7x, 32 devices: a whole 2x2x4 slice. The times are simulated.
32 devices in a mesh: wide: 16 (over z, x, core), narrow: 2 (over y).
Axes of the slice: x: 2, y: 2, z: 4, core: 2. Of those that a mesh axis runs over, the one named last changes fastest.
Arguments:
- tokens: bfloat16 [128, 196, 768], P('wide'), may hold values from -6 to 6
- merge_map: int32 [128, 196], P('wide'), may hold values from 0 to 195, as said below
- counts: int32 [128], P('wide'), may hold values from 60 to 196, as said below
- ln_gain: float32 [2, 768], replicated, may hold values from 0.1 to 1.9
- w_qkv: bfloat16 [2, 3, 768, 768], P(None, None, None, 'narrow'), may hold values from -0.21875 to 0.21875
- qk_gain: float32 [2, 2, 64], replicated, may hold values from 0.1 to 1.9
- w_out: bfloat16 [2, 768, 768], P(None, 'narrow'), may hold values from -0.625 to 0.625
- w_up: bfloat16 [2, 768, 3072], P(None, None, 'narrow'), may hold values from -0.21875 to 0.21875
- b_up: bfloat16 [2, 3072], P(None, 'narrow'), may hold values from -3 to 3
- w_down: bfloat16 [2, 3072, 768], P(None, 'narrow'), may hold values from -0.109375 to 0.109375
- b_down: float32 [2, 768], replicated, may hold values from -2 to 2
- cotangent: bfloat16 [128, 196, 768], P('wide'), may hold values from -6 to 6
Outputs:
- first_out: float32 [128, 196, 768], P('wide')
- second_out: float32 [128, 196, 768], P('wide')
- grad_tokens: float32 [128, 196, 768], P('wide')
- grad_ln_gain: float32 [2, 768], replicated
- grad_qkv: float32 [2, 3, 768, 768], P(None, None, None, 'narrow')
- grad_qk_gain: float32 [2, 2, 64], replicated
- grad_out: float32 [2, 768, 768], P(None, 'narrow')
- grad_up: float32 [2, 768, 3072], P(None, None, 'narrow')
- grad_b_up: float32 [2, 3072], P(None, 'narrow')
- grad_down: float32 [2, 3072, 768], P(None, 'narrow')
- grad_b_down: float32 [2, 768], replicated
Inputs may be any that keep to these rules, and one draw needn't show every extreme that they name: `counts`: each image's live tokens fill its first slots; at least one image has 196 live tokens and at least one has 60. merge_map[i, p] names the live token of image i (below counts[i]) into which patch p was merged; every live token of an image is named by at least one patch.
All inputs are finite; a program needn't handle non-finite values.
Results may differ from a plain program's by a relative error of at most 0.022.
Values may be sent and summed in bfloat16 or wider, within the bound.
No kernel may reach another device: no remote copies, remote signals or barrier semaphores. Data moves between devices by JAX's collectives and lax.ppermute only.
A program may use at most 320 MiB of HBM per device.

v0:
```python
import jax
import jax.numpy as jnp
from jax import lax
from jax.sharding import PartitionSpec as P


def shifted_2(value, axis, by):
    length = lax.axis_size(axis)
    pairs = [(i, i + by) for i in range(length) if 0 <= i + by < length]
    return lax.ppermute(value, axis, pairs)


def norm_rows(inputs, gain_row):
    centre = jnp.mean(inputs, axis=-1, keepdims=True)
    centered = inputs - centre
    inverse = lax.rsqrt(jnp.mean(centered * centered, axis=-1, keepdims=True) + 1e-06)
    normal = centered * inverse
    return (normal, inverse, normal * gain_row)


def norm_back(upstream, normal, inverse, gain_row):
    scaled = upstream * gain_row
    return inverse * (
        scaled
        - jnp.mean(scaled, axis=-1, keepdims=True)
        - normal * jnp.mean(scaled * normal, axis=-1, keepdims=True)
    )


def attend(normed_low, key_bias, qkv_full, out_full, qk_gains):
    head_dim = qk_gains.shape[-1]
    head_count = qkv_full.shape[-1] // head_dim
    qkv_heads = qkv_full.reshape(3, qkv_full.shape[1], head_count, head_dim)
    projected = jnp.einsum(
        "bsd,kdhe->kbhse", normed_low, qkv_heads, preferred_element_type=jnp.float32
    )
    q_normal, q_inverse, queries = norm_rows(projected[0], qk_gains[0])
    k_normal, k_inverse, keys_normed = norm_rows(projected[1], qk_gains[1])
    queries_low = queries.astype(jnp.bfloat16)
    keys_low = keys_normed.astype(jnp.bfloat16)
    values_low = projected[2].astype(jnp.bfloat16)
    score_scale = head_dim ** (-0.5)
    scores = jnp.einsum(
        "bhse,bhte->bhst", queries_low, keys_low, preferred_element_type=jnp.float32
    )
    logits = scores * score_scale + key_bias[:, None, None, :]
    shifted = jnp.exp(logits - jnp.max(logits, axis=-1, keepdims=True))
    softened = shifted / jnp.sum(shifted, axis=-1, keepdims=True)
    soft_low = softened.astype(jnp.bfloat16)
    mixed_low = jnp.einsum(
        "bhst,bhte->bhse", soft_low, values_low, preferred_element_type=jnp.float32
    ).astype(jnp.bfloat16)
    out_heads = out_full.reshape(head_count, head_dim, out_full.shape[-1])
    branch = jnp.einsum("bhse,hed->bsd", mixed_low, out_heads, preferred_element_type=jnp.float32)
    kept_parts = (
        q_normal,
        q_inverse,
        k_normal,
        k_inverse,
        queries_low,
        keys_low,
        values_low,
        softened,
        soft_low,
        mixed_low,
        qkv_heads,
        out_heads,
        score_scale,
    )
    return (branch, kept_parts)


def attend_back(normed_low, key_bias, qkv_full, out_full, qk_gains, grad_low):
    branch, kept_parts = attend(normed_low, key_bias, qkv_full, out_full, qk_gains)
    (
        q_normal,
        q_inverse,
        k_normal,
        k_inverse,
        queries_low,
        keys_low,
        values_low,
        softened,
        soft_low,
        mixed_low,
        qkv_heads,
        out_heads,
        score_scale,
    ) = kept_parts
    d_mixed = jnp.einsum(
        "bsd,hed->bhse", grad_low, out_heads, preferred_element_type=jnp.float32
    ).astype(jnp.bfloat16)
    g_out = jnp.einsum(
        "bhse,bsd->hed", mixed_low, grad_low, preferred_element_type=jnp.float32
    ).reshape(out_full.shape)
    d_soft = jnp.einsum("bhse,bhte->bhst", d_mixed, values_low, preferred_element_type=jnp.float32)
    row_dot = jnp.sum(softened * d_soft, axis=-1, keepdims=True)
    d_scores = (softened * (d_soft - row_dot) * score_scale).astype(jnp.bfloat16)
    d_queries = jnp.einsum(
        "bhst,bhte->bhse", d_scores, keys_low, preferred_element_type=jnp.float32
    )
    d_keys = jnp.einsum(
        "bhst,bhse->bhte", d_scores, queries_low, preferred_element_type=jnp.float32
    )
    d_values = jnp.einsum("bhst,bhse->bhte", soft_low, d_mixed, preferred_element_type=jnp.float32)
    g_gains = jnp.stack(
        [jnp.sum(d_queries * q_normal, axis=(0, 1, 2)), jnp.sum(d_keys * k_normal, axis=(0, 1, 2))]
    )
    d_projected = jnp.stack(
        [
            norm_back(d_queries, q_normal, q_inverse, qk_gains[0]),
            norm_back(d_keys, k_normal, k_inverse, qk_gains[1]),
            d_values,
        ]
    ).astype(jnp.bfloat16)
    g_qkv = jnp.einsum(
        "bsd,kbhse->kdhe", normed_low, d_projected, preferred_element_type=jnp.float32
    ).reshape(qkv_full.shape)
    d_normed = jnp.einsum(
        "kbhse,kdhe->bsd", d_projected, qkv_heads, preferred_element_type=jnp.float32
    )
    return (d_normed, g_qkv, g_out, g_gains)


def expand(normed_low, up_full, bias_full, down_full):
    pre_act = jnp.einsum(
        "bsd,df->bsf", normed_low, up_full, preferred_element_type=jnp.float32
    ) + bias_full.astype(jnp.float32)
    hidden, gelu_back = jax.vjp(jax.nn.gelu, pre_act)
    hidden_low = hidden.astype(jnp.bfloat16)
    branch = jnp.einsum("bsf,fd->bsd", hidden_low, down_full, preferred_element_type=jnp.float32)
    return (branch, hidden_low, gelu_back)


def expand_back(normed_low, up_full, bias_full, down_full, grad_low):
    branch, hidden_low, gelu_back = expand(normed_low, up_full, bias_full, down_full)
    d_hidden = jnp.einsum("bsd,fd->bsf", grad_low, down_full, preferred_element_type=jnp.float32)
    d_pre = gelu_back(d_hidden)[0].astype(jnp.bfloat16)
    g_bias = jnp.sum(d_pre, axis=(0, 1), dtype=jnp.float32)
    g_up = jnp.einsum("bsd,bsf->df", normed_low, d_pre, preferred_element_type=jnp.float32)
    g_down = jnp.einsum("bsf,bsd->fd", hidden_low, grad_low, preferred_element_type=jnp.float32)
    d_normed = jnp.einsum("bsf,df->bsd", d_pre, up_full, preferred_element_type=jnp.float32)
    return (d_normed, g_up, g_bias, g_down)


def body(
    tokens, merge_map, counts, ln_gain, w_qkv, qk_gain, w_out, w_up, b_up, w_down, b_down, cotangent
):
    pair_gap = lax.axis_size("narrow") // 2
    on_attention = lax.axis_index("narrow") < pair_gap
    layers = ln_gain.shape[0]
    col_half = w_qkv.shape[-1]
    unit_half = w_up.shape[-1]
    model_dim = tokens.shape[-1]
    slot_ids = jnp.arange(tokens.shape[1], dtype=jnp.int32)
    live_rows = slot_ids[None, :] < counts[:, None]
    row_weight = jnp.where(live_rows, 1.0, 0.0).astype(jnp.float32)[:, :, None]
    merged_sizes = jnp.sum(
        jnp.where(merge_map[:, :, None] == slot_ids[None, None, :], 1.0, 0.0), axis=1
    ).astype(jnp.float32)
    key_bias = jnp.where(live_rows, jnp.log(jnp.where(live_rows, merged_sizes, 1.0)), -1e30)
    attn_far = shifted_2((w_qkv, w_out), "narrow", -pair_gap)
    mlp_far = shifted_2((w_up, b_up, w_down), "narrow", pair_gap)

    def attention_weights(layer_at):
        qkv_full = jnp.concatenate([w_qkv[layer_at], attn_far[0][layer_at]], axis=-1)
        out_full = jnp.concatenate([w_out[layer_at], attn_far[1][layer_at]], axis=0)
        return (qkv_full, out_full)

    def feed_weights(layer_at):
        up_full = jnp.concatenate([mlp_far[0][layer_at], w_up[layer_at]], axis=-1)
        bias_full = jnp.concatenate([mlp_far[1][layer_at], b_up[layer_at]], axis=-1)
        down_full = jnp.concatenate([mlp_far[2][layer_at], w_down[layer_at]], axis=0)
        return (up_full, bias_full, down_full)

    current = tokens.astype(jnp.float32)
    layer_inputs = []
    outputs = []
    for layer_at in range(layers):
        normal, inverse, normed = norm_rows(current, ln_gain[layer_at])
        normed_low = normed.astype(jnp.bfloat16)

        def attention_forward():
            qkv_full, out_full = attention_weights(layer_at)
            return attend(normed_low, key_bias, qkv_full, out_full, qk_gain[layer_at])[0]

        def feed_forward():
            up_full, bias_full, down_full = feed_weights(layer_at)
            return expand(normed_low, up_full, bias_full, down_full)[0]

        partial_value = lax.cond(on_attention, attention_forward, feed_forward)
        layer_inputs.append(current)
        branch_total = lax.psum(partial_value, "narrow")
        current = row_weight * (current + branch_total + b_down[layer_at])
        outputs.append(current)
    grad_rows = cotangent.astype(jnp.float32)
    collected = []
    for layer_at in reversed(range(layers)):
        normal, inverse, normed = norm_rows(layer_inputs[layer_at], ln_gain[layer_at])
        normed_low = normed.astype(jnp.bfloat16)
        masked_grad = row_weight * grad_rows
        grad_low = masked_grad.astype(jnp.bfloat16)

        def attention_side():
            qkv_full, out_full = attention_weights(layer_at)
            d_normed, g_qkv, g_out, g_gains = attend_back(
                normed_low, key_bias, qkv_full, out_full, qk_gain[layer_at], grad_low
            )
            return (
                d_normed,
                g_gains,
                g_qkv,
                g_out,
                jnp.zeros((model_dim, 2 * unit_half), jnp.float32),
                jnp.zeros((2 * unit_half,), jnp.float32),
                jnp.zeros((2 * unit_half, model_dim), jnp.float32),
            )

        def feed_side():
            up_full, bias_full, down_full = feed_weights(layer_at)
            d_normed, g_up, g_bias, g_down = expand_back(
                normed_low, up_full, bias_full, down_full, grad_low
            )
            return (
                d_normed,
                jnp.zeros(qk_gain[layer_at].shape, jnp.float32),
                jnp.zeros((3, model_dim, 2 * col_half), jnp.float32),
                jnp.zeros((2 * col_half, model_dim), jnp.float32),
                g_up,
                g_bias,
                g_down,
            )

        returned = lax.cond(on_attention, attention_side, feed_side)
        d_normed, g_gains = (
            lax.psum(returned[0].astype(jnp.bfloat16), "narrow").astype(jnp.float32),
            lax.psum(returned[1].astype(jnp.bfloat16), "narrow").astype(jnp.float32),
        )
        g_ln = jnp.sum(d_normed * normal, axis=(0, 1))
        grad_rows = masked_grad + norm_back(d_normed, normal, inverse, ln_gain[layer_at])
        qkv_far, out_far = (
            shifted_2(returned[2][..., col_half:].astype(jnp.bfloat16), "narrow", pair_gap).astype(
                jnp.float32
            ),
            shifted_2(returned[3][col_half:].astype(jnp.bfloat16), "narrow", pair_gap).astype(
                jnp.float32
            ),
        )
        up_far, bias_far, down_far = (
            shifted_2(returned[4][:, :unit_half].astype(jnp.bfloat16), "narrow", -pair_gap).astype(
                jnp.float32
            ),
            shifted_2(returned[5][:unit_half].astype(jnp.bfloat16), "narrow", -pair_gap).astype(
                jnp.float32
            ),
            shifted_2(returned[6][:unit_half].astype(jnp.bfloat16), "narrow", -pair_gap).astype(
                jnp.float32
            ),
        )
        own_qkv = jnp.where(on_attention, returned[2][..., :col_half], qkv_far)
        own_out = jnp.where(on_attention, returned[3][:col_half], out_far)
        own_up = jnp.where(on_attention, up_far, returned[4][:, unit_half:])
        own_bias = jnp.where(on_attention, bias_far, returned[5][unit_half:])
        own_down = jnp.where(on_attention, down_far, returned[6][unit_half:])
        g_bdown = jnp.sum(masked_grad, axis=(0, 1))
        shards = (own_qkv, own_out, own_up, own_bias, own_down, g_ln, g_gains, g_bdown)
        collected.append(shards)
    collected = collected[::-1]
    stacked = tuple(
        (jnp.stack([element[position] for element in collected]) for position in range(8))
    )
    stacked = (
        lax.psum(stacked[0].astype(jnp.bfloat16), "wide").astype(jnp.float32),
        lax.psum(stacked[1].astype(jnp.bfloat16), "wide").astype(jnp.float32),
        lax.psum(stacked[2].astype(jnp.bfloat16), "wide").astype(jnp.float32),
        lax.psum(stacked[3].astype(jnp.bfloat16), "wide").astype(jnp.float32),
        lax.psum(stacked[4].astype(jnp.bfloat16), "wide").astype(jnp.float32),
        lax.psum(stacked[5].astype(jnp.bfloat16), "wide").astype(jnp.float32),
        lax.psum(stacked[6].astype(jnp.bfloat16), "wide").astype(jnp.float32),
        lax.psum(stacked[7].astype(jnp.bfloat16), "wide").astype(jnp.float32),
    )
    return (
        outputs[0],
        outputs[-1],
        grad_rows,
        stacked[5],
        stacked[0],
        stacked[6],
        stacked[1],
        stacked[2],
        stacked[3],
        stacked[4],
        stacked[7],
    )


def solution(mesh):
    placed = (
        P("wide", None, None),
        P("wide", None),
        P("wide"),
        P(),
        P(None, None, None, "narrow"),
        P(),
        P(None, "narrow", None),
        P(None, None, "narrow"),
        P(None, "narrow"),
        P(None, "narrow", None),
        P(),
        P("wide", None, None),
    )
    return jax.shard_map(
        body,
        mesh=mesh,
        in_specs=placed,
        out_specs=(
            P("wide", None, None),
            P("wide", None, None),
            P("wide", None, None),
            P(),
            P(None, None, None, "narrow"),
            P(),
            P(None, "narrow", None),
            P(None, None, "narrow"),
            P(None, "narrow"),
            P(None, "narrow", None),
            P(),
        ),
        check_vma=False,
    )
```

profile of v0, /device:TPU:0, one launch (start us, length us, event | category | flops | bytes accessed | tf_op | source)
XLA Modules:
  0.0 1558.4 jit_solution(15057311428997146652)
XLA Ops:
  7.2 7.0 collective-permute-start
  17.7 6.0 copy.130
  26.3 8.0 collective-permute-start.1
  42.9 86.2 %collective-permute-done.4 = bf16[2,384,768]{2,1,0:T(8,128)(2,1)} collective-permute-done((bf16[2,384,768]{2,1,0:T(8,128)(2,1)}, bf16[2,384,768]{2,1,0:T(8,128)(2,1)}, u32[]{:S(2)}, u32[]{:S(2)}) %collective-permute-start.4) | collective-permute-done | bytes 1179680 | tf_op jit(solution)/shard_map/ppermute | solution.py:10
  129.1 85.5 %collective-permute-done.1 = bf16[2,1536]{1,0:T(2,128)(2,1)} collective-permute-done((bf16[2,1536]{1,0:T(2,128)(2,1)S(1)}, bf16[2,1536]{1,0:T(2,128)(2,1)}, u32[]{:S(2)}, u32[]{:S(2)}) %collective-permute-start.1) | collective-permute-done | bytes 6176 | tf_op jit(solution)/shard_map/ppermute | solution.py:10
  214.7 66.7 %conditional.4 = (f32[8,196,768]{2,1,0:T(8,128)}) conditional(s32[]{:T(128)} %convert_element_type.255, (bf16[2,768,1536]{2,1,0:T(8,128)(2,1)}, bf16[2,768,1536]{2,1,0:T(8,128)(2,1)}, bf16[8,196,768]{2,0,1:T(8,128)(2,1)}, bf16[2,1536]{1,0:T(2,128)(2,1)}, bf16[2,1536]{1,0:T(2,128)(2,1)S(1)}, /*index=5*/bf16[2,1536,768]{2,1,0:T(8,128)(2,1)}, ...), branch_computations={%region_3.4_spmd, %region_4.11_spmd} | conditional | flops 14864560128 | bytes 182532832 | solution.py:191
  230.2 9.9 convolution_bitcast_fusion
  246.5 5.1 multiply_convert_fusion.1
  251.7 14.0 fusion.376
  268.1 13.1 fusion.29
  281.4 6.2 copy.135
  290.4 118.9 %all-reduce.9.cloned.1.call-done = f32[8,196,768]{2,0,1:T(8,128)} async-done(((f32[8,196,768]{2,0,1:T(8,128)}), f32[8,196,768]{2,0,1:T(8,128)}) %all-reduce.9.cloned.1.call-update) | async-done | bytes 4816912 | tf_op jit(solution)/shard_map/psum | solution.py:193
  409.4 5.6 fusion.374
  418.1 203.0 %conditional.6 = (bf16[8,196,768]{2,1,0:T(8,128)(2,1)}, bf16[2,64]{1,0:T(2,128)(2,1)}, bf16[768,768]{1,0:T(8,128)(2,1)}, bf16[768,3072]{1,0:T(8,128)(2,1)}, bf16...) conditional(s32[]{:T(128)} %convert_element_type.255, ...), branch_computations={%region_23.25_spmd, %region_25.39_spmd} | conditional | flops 37181038592 | bytes 392862944 | solution.py:234
  435.6 9.9 convolution_bitcast_fusion.2
  453.7 5.3 multiply_convert_fusion.8
  459.0 13.8 fusion.394
  474.2 5.7 convert_bitcast_fusion.1
  479.9 25.3 %multiply_convert_fusion.4 = bf16[8,12,196,196]{2,3,1,0:T(8,128)(2,1)} fusion(bf16[8,12,196,64]{2,3,0,1:T(8,128)(2,1)} %convert_bitcast_fusion.1, f32[8,12,196,196]{2,3,1,0:T(8,128)} %get-tuple-element.460, f32[8,12,196]{2,1,0:T(8,128)} %get-tuple-element.459, f32[3,8,12,196,64]{3,4,1,2,0:T(8,128)} %copy-done), kind=kOutput, calls=%fused_computation.90 | convolution fusion | flops 969946176 | bytes 59542528 | tf_op jit(solution)/shard_map/cond/branch_1_fun/sub | solution.py:98
  505.2 10.6 fusion.86
  515.9 16.0 %multiply_reduce_fusion.6 = (bf16[64]{0:T(256)(128)(2,1)S(1)}, f32[8,12,196]{2,0,1:T(8,128)}, f32[8,12,196]{2,0,1:T(8,128)}, bf16[64]{0:T(256)(128)(2,1)S(1)}, f...) fusion(f32[8,12,196]{2,0,1:T(8,128)} %copy-done.31, f32[8,12,196]{2,0,1:T(8,128)} %copy-done.28, ...), kind=kOutput, calls=%fused_computation.115 | convolution fusion | flops 491248000 | bytes 29654784 | tf_op jit(solution)/shard_map/cond/branch_1_fun/bhst,bhte->bhse/dot_general | solution.py:99
  535.5 13.5 fusion.98
  549.0 12.4 fusion.149
  561.4 9.6 convert_bitcast_fusion
  571.0 12.5 fusion.138
  583.5 6.0 copy.221
  593.0 10.8 fusion.128
  603.9 11.2 fusion.101
  624.8 62.9 %conditional.5 = (f32[8,196,768]{2,1,0:T(8,128)}) conditional(s32[]{:T(128)} %convert_element_type.255, (bf16[2,768,1536]{2,1,0:T(8,128)(2,1)}, bf16[2,768,1536]{2,1,0:T(8,128)(2,1)}, bf16[8,196,768]{2,0,1:T(8,128)(2,1)}, bf16[2,1536]{1,0:T(2,128)(2,1)}, bf16[2,1536]{1,0:T(2,128)(2,1)S(1)}, /*index=5*/bf16[2,1536,768]{2,1,0:T(8,128)(2,1)}, ...), branch_computations={%region_14.15_spmd, %region_15.22_spmd} | conditional | flops 14864560128 | bytes 182528704 | solution.py:191
  636.1 9.8 convolution_bitcast_fusion.1
  652.5 5.1 multiply_convert_fusion.3
  657.6 14.4 fusion.385
  674.4 13.1 fusion.65
  687.6 6.2 copy.139
  708.3 9.1 collective-permute-start.6
  719.4 5.1 fusion.356
  725.2 183.5 %all-reduce.11.cloned.1.call-done = f32[8,196,768]{2,0,1:T(8,128)} async-done(((f32[8,196,768]{2,0,1:T(8,128)}), f32[8,196,768]{2,0,1:T(8,128)}) %all-reduce.11.cloned.1.call-update) | async-done | bytes 4816912 | tf_op jit(solution)/shard_map/psum | solution.py:193
  908.7 10.0 fusion.372
  921.7 188.4 %conditional.7 = (bf16[8,196,768]{2,1,0:T(8,128)(2,1)}, bf16[2,64]{1,0:T(2,128)(2,1)S(1)}, bf16[768,768]{1,0:T(8,128)(2,1)}, bf16[768,3072]{1,0:T(8,128)(2,1)}, ...) conditional(s32[]{:T(128)} %convert_element_type.255, ...), branch_computations={%region_42.44_spmd, %region_44.58_spmd} | conditional | flops 37181038592 | bytes 436657888 | solution.py:234
  938.0 10.0 convolution_bitcast_fusion.3
  954.6 4.6 multiply_convert_fusion.13
  959.1 13.5 fusion.403
  974.0 5.7 convert_bitcast_fusion.3
  979.8 25.2 %multiply_convert_fusion.9 = bf16[8,12,196,196]{2,3,1,0:T(8,128)(2,1)} fusion(bf16[8,12,196,64]{2,3,0,1:T(8,128)(2,1)} %convert_bitcast_fusion.3, f32[8,12,196,196]{2,3,1,0:T(8,128)} %get-tuple-element.473, f32[8,12,196]{2,1,0:T(8,128)} %get-tuple-element.472, f32[3,8,12,196,64]{3,4,1,2,0:T(8,128)} %copy-done.1), kind=kOutput, calls=%fused_computation.181 | convolution fusion | flops 969946176 | bytes 59542528 | tf_op jit(solution)/shard_map/cond/branch_1_fun/sub | solution.py:98
  1004.9 9.7 fusion.164
  1014.7 15.3 multiply_reduce_fusion.15
  1030.0 12.7 fusion.176
  1042.7 13.6 fusion.227
  1056.3 9.6 convert_bitcast_fusion.2
  1065.9 12.1 fusion.216
  1077.9 4.3 copy.223
  1084.5 11.1 fusion.206
  1095.6 11.2 fusion.179
  1118.3 6.6 collective-permute-start.5
  1133.4 6.8 collective-permute-start.7
  1140.2 4.4 fusion.364
  1148.3 47.7 %collective-permute-done.7 = bf16[384,768]{1,0:T(8,128)(2,1)} collective-permute-done((bf16[384,768]{1,0:T(8,128)(2,1)S(1)}, bf16[384,768]{1,0:T(8,128)(2,1)}, u32[]{:S(2)}, u32[]{:S(2)}) %collective-permute-start.7) | collective-permute-done | bytes 589856 | tf_op jit(solution)/shard_map/ppermute | solution.py:10
  1208.7 60.7 %collective-permute-done.9 = bf16[768,1536]{1,0:T(8,128)(2,1)} collective-permute-done((bf16[768,1536]{1,0:T(8,128)(2,1)}, bf16[768,1536]{1,0:T(8,128)(2,1)}, u32[]{:S(2)}, u32[]{:S(2)}) %collective-permute-start.9) | collective-permute-done | bytes 2359328 | tf_op jit(solution)/shard_map/ppermute | solution.py:10
  1283.5 5.5 all-reduce.2
  1293.0 61.4 %all-reduce = (bf16[2,768]{1,0:T(2,128)(2,1)S(1)}, bf16[2,2,64]{2,1,0:T(2,128)(2,1)S(1)}, bf16[2,1536]{1,0:T(2,128)(2,1)S(1)}, bf16[2,768]{1,0:T(2,128)(2,1)S(1)}) all-reduce(bf16[2,768]{1,0:T(2,128)(2,1)S(1)} %pad_maximum_fusion.19, bf16[2,2,64]{2,1,0:T(2,128)(2,1)S(1)} %pad_maximum_fusion.21, ...), channel_id=1, replica_groups=mesh['wide'=16,'narrow'=2] {'wide'}, use_global_device_ids=true, to_apply=%region_63.64 | all-reduce | flops 6400 | bytes 25600 | tf_op jit(solution)/shard_map/psum | solution.py:278
  1356.8 5.5 fusion.349
  1362.3 172.3 %all-reduce.17.cloned.1.call-done = (bf16[2,3,768,384]{3,2,1,0:T(8,128)(2,1)}, bf16[2,384,768]{2,1,0:T(8,128)(2,1)}, bf16[2,768,1536]{2,1,0:T(8,128)(2,1)}, bf16[2,1536,768]{2,1,0:T(8,128)(2,1)}) async-done(((bf16[2,3,768,384]{3,2,1,0:T(8,128)(2,1)}, bf16[2,384,768]{2,1,0:T(8,128)(2,1)}, bf16[2,768,1536]{2,1,0:T(8,128)(2,1)}, bf16[2,1536,768]{2,1,0:T(8,128)(2,1)}), (bf16[2,3,768,384]{3,2,1,0:T(8,128)(2,1)}, ...) | async-done | bytes 14155792 | tf_op jit(solution)/shard_map/psum | solution.py:273
  1534.6 7.6 convert_element_type.277
  1542.1 4.5 convert_element_type.283
  (283 shorter events, 185.1 us)
Async XLA Ops:
  7.2 19.1 %copy-start.34 = (bf16[2,1536]{1,0:T(2,128)(2,1)S(1)}, bf16[2,1536]{1,0:T(2,128)(2,1)}, u32[]{:S(2)}) copy-start(bf16[2,1536]{1,0:T(2,128)(2,1)} %param.28) | copy-start | bytes 18436
  7.2 27.1 %copy-start.47 = (s32[8,196]{1,0:T(8,128)S(1)}, s32[8,196]{1,0:T(8,128)}, u32[]{:S(2)}) copy-start(s32[8,196]{1,0:T(8,128)} %param.21) | copy-start | bytes 18820
  7.2 402.2 %all-reduce.9.cloned.1.call-start = ((), (), s32[]{:S(2)}) async-start(), calls=%async_computation | async-start | bytes 9633792 | tf_op jit(solution)/shard_map/psum | solution.py:193
  7.2 207.4 %collective-permute-start = (bf16[2,768,1536]{2,1,0:T(8,128)(2,1)}, bf16[2,768,1536]{2,1,0:T(8,128)(2,1)}, u32[]{:S(2)}, u32[]{:S(2)}) collective-permute-start(bf16[2,768,1536]{2,1,0:T(8,128)(2,1)} %param.27), channel_id=1, source_target_pairs={{0,1},{2,3},{4,5},{6,7},{8,9},{10,11},{12,13},{14,15},{16,17},{18,... | collective-permute-start | bytes 14155784 | tf_op jit(solution)/shard_map/ppermute | solution.py:10
  14.2 200.5 %collective-permute-start.2 = (bf16[2,1536,768]{2,1,0:T(8,128)(2,1)}, bf16[2,1536,768]{2,1,0:T(8,128)(2,1)}, u32[]{:S(2)}, u32[]{:S(2)}) collective-permute-start(bf16[2,1536,768]{2,1,0:T(8,128)(2,1)} %param.29), channel_id=1, source_target_pairs={{0,1},{2,3},{4,5},{6,7},{8,9},{10,11},{12,13},{14,15},{16,17},{18,... | collective-permute-start | bytes 14155784 | tf_op jit(solution)/shard_map/ppermute | solution.py:10
  23.7 105.5 %collective-permute-start.3 = (bf16[2,3,768,384]{2,3,1,0:T(8,128)(2,1)}, bf16[2,3,768,384]{2,3,1,0:T(8,128)(2,1)}, u32[]{:S(2)}, u32[]{:S(2)}) collective-permute-start(bf16[2,3,768,384]{2,3,1,0:T(8,128)(2,1)} %copy.130), channel_id=1, source_target_pairs={{1,0},{3,2},{5,4},{7,6},{9,8},{11,10},{13,12},{15,14},{17,16},{19,... | collective-permute-start | bytes 10616840 | tf_op jit(solution)/shard_map/ppermute | solution.py:10
  25.0 104.2 %collective-permute-start.4 = (bf16[2,384,768]{2,1,0:T(8,128)(2,1)}, bf16[2,384,768]{2,1,0:T(8,128)(2,1)}, u32[]{:S(2)}, u32[]{:S(2)}) collective-permute-start(bf16[2,384,768]{2,1,0:T(8,128)(2,1)} %param.26), channel_id=1, source_target_pairs={{1,0},{3,2},{5,4},{7,6},{9,8},{11,10},{13,12},{15,14},{17,16},{19,... | collective-permute-start | bytes 3538952 | tf_op jit(solution)/shard_map/ppermute | solution.py:10
  26.3 188.4 %collective-permute-start.1 = (bf16[2,1536]{1,0:T(2,128)(2,1)S(1)}, bf16[2,1536]{1,0:T(2,128)(2,1)}, u32[]{:S(2)}, u32[]{:S(2)}) collective-permute-start(bf16[2,1536]{1,0:T(2,128)(2,1)S(1)} %copy-done.34), channel_id=1, source_target_pairs={{0,1},{2,3},{4,5},{6,7},{8,9},{10,11},{12,13},{14,15},{16,17},{18,... | collective-permute-start | bytes 18440 | tf_op jit(solution)/shard_map/ppermute | solution.py:10
  34.4 5.9 copy-start.4
  34.7 7.6 copy-start.57
  34.7 180.0 %copy-start.3 = (bf16[2,3,768,384]{3,2,1,0:T(8,128)(2,1)S(1)}, bf16[2,3,768,384]{3,2,1,0:T(8,128)(2,1)}, u32[]{:S(2)}) copy-start(bf16[2,3,768,384]{3,2,1,0:T(8,128)(2,1)} %param.24) | copy-start | bytes 10616836
  36.9 5.3 copy-start.17
  37.7 176.9 %copy-start.40 = (f32[768]{0:T(1024)}, f32[768]{0:T(1024)S(1)}, u32[]{:S(2)}) copy-start(f32[768]{0:T(1024)S(1)} %get-tuple-element.418) | copy-start | bytes 9220
  37.8 377.9 %copy-start.38 = (f32[768]{0:T(1024)}, f32[768]{0:T(1024)S(1)}, u32[]{:S(2)}) copy-start(f32[768]{0:T(1024)S(1)} %get-tuple-element.417) | copy-start | bytes 9220
  240.1 6.5 copy-start.6
  246.5 5.1 copy-start.49
  287.6 431.7 %all-reduce.13.cloned.1.call-start = ((), (), s32[]{:S(2)}) async-start(), calls=%async_computation.2 | async-start | bytes 4816896 | tf_op jit(solution)/shard_map/psum | solution.py:236
  432.2 13.3 copy-start.21
  445.5 8.1 copy-start
  453.5 5.5 copy-start.30
  453.6 5.4 copy-start.31
  453.6 5.4 copy-start.50
  535.4 13.5 copy-start.32
  621.0 3.7 copy-start.36
  624.7 284.0 %all-reduce.11.cloned.1.call-start = ((), (), s32[]{:S(2)}) async-start(), calls=%async_computation.1 | async-start | bytes 9633792 | tf_op jit(solution)/shard_map/psum | solution.py:193
  646.0 6.5 copy-start.7
  652.5 5.1 copy-start.51
  693.8 595.3 %all-reduce.15.cloned.1.call-start = ((), (), s32[]{:S(2)}) async-start(), calls=%async_computation.3 | async-start | bytes 4816896 | tf_op jit(solution)/shard_map/psum | solution.py:236
  695.0 22.4 %collective-permute-start.8 = (bf16[384,768]{1,0:T(8,128)(2,1)S(1)}, bf16[384,768]{1,0:T(8,128)(2,1)S(1)}, u32[]{:S(2)}, u32[]{:S(2)}) collective-permute-start(bf16[384,768]{1,0:T(8,128)(2,1)S(1)} %slice.498), channel_id=1, source_target_pairs={{0,1},{2,3},{4,5},{6,7},{8,9},{10,11},{12,13},{14,15},{16,17},{18,... | collective-permute-start | bytes 1769480 | tf_op jit(solution)/shard_map/ppermute | solution.py:10
  699.6 425.3 %collective-permute-start.14 = (bf16[1536,768]{1,0:T(8,128)(2,1)}, bf16[1536,768]{1,0:T(8,128)(2,1)}, u32[]{:S(2)}, u32[]{:S(2)}) collective-permute-start(bf16[1536,768]{1,0:T(8,128)(2,1)} %slice.492), channel_id=1, source_target_pairs={{1,0},{3,2},{5,4},{7,6},{9,8},{11,10},{13,12},{15,14},{17,16},{19,... | collective-permute-start | bytes 7077896 | tf_op jit(solution)/shard_map/ppermute | solution.py:10
  700.9 18.5 %copy-start.39 = (f32[768]{0:T(1024)S(1)}, f32[768]{0:T(1024)}, u32[]{:S(2)}) copy-start(f32[768]{0:T(1024)} %copy-done.38) | copy-start | bytes 9220
  704.1 436.1 %collective-permute-start.10 = (bf16[768,1536]{1,0:T(8,128)(2,1)}, bf16[768,1536]{1,0:T(8,128)(2,1)}, u32[]{:S(2)}, u32[]{:S(2)}) collective-permute-start(bf16[768,1536]{1,0:T(8,128)(2,1)} %slice.494), channel_id=1, source_target_pairs={{1,0},{3,2},{5,4},{7,6},{9,8},{11,10},{13,12},{15,14},{17,16},{19,... | collective-permute-start | bytes 7077896 | tf_op jit(solution)/shard_map/ppermute | solution.py:10
  708.3 200.4 %copy-start.43 = (f32[768]{0:T(1024)S(1)}, f32[768]{0:T(1024)}, u32[]{:S(2)}) copy-start(f32[768]{0:T(1024)} %get-tuple-element.415) | copy-start | bytes 9220
  708.3 404.8 %collective-permute-start.6 = (bf16[3,768,384]{2,1,0:T(8,128)(2,1)}, bf16[3,768,384]{2,1,0:T(8,128)(2,1)}, u32[]{:S(2)}, u32[]{:S(2)}) collective-permute-start(bf16[3,768,384]{2,1,0:T(8,128)(2,1)} %slice.496), channel_id=1, source_target_pairs={{0,1},{2,3},{4,5},{6,7},{8,9},{10,11},{12,13},{14,15},{16,17},{18,... | collective-permute-start | bytes 5308424 | tf_op jit(solution)/shard_map/ppermute | solution.py:10
  935.8 12.3 copy-start.22
  938.0 10.1 copy-start.23
  948.1 6.5 copy-start.1
  1030.0 12.7 copy-start.33
  1042.7 23.2 %copy-start.16 = (bf16[1,8,12,196,64]{3,4,1,2,0:T(8,128)(2,1)}, bf16[1,8,12,196,64]{3,4,1,2,0:T(8,128)(2,1)S(1)}, u32[]{:S(2)}) copy-start(bf16[1,8,12,196,64]{3,4,1,2,0:T(8,128)(2,1)S(1)} %get-tuple-element.466) | copy-start | bytes 7225348 | tf_op jit(solution)/shard_map/cond
  1082.2 13.3 copy-start.9
  1110.1 6.7 copy-start.14
  1110.1 6.7 copy-start.59
  1111.8 92.0 %collective-permute-start.13 = (bf16[1536,768]{1,0:T(8,128)(2,1)}, bf16[1536,768]{1,0:T(8,128)(2,1)}, u32[]{:S(2)}, u32[]{:S(2)}) collective-permute-start(bf16[1536,768]{1,0:T(8,128)(2,1)} %slice.493), channel_id=1, source_target_pairs={{1,0},{3,2},{5,4},{7,6},{9,8},{11,10},{13,12},{15,14},{17,16},{19,... | collective-permute-start | bytes 7077896 | tf_op jit(solution)/shard_map/ppermute | solution.py:10
  1118.3 80.3 %collective-permute-start.5 = (bf16[3,768,384]{2,1,0:T(8,128)(2,1)}, bf16[3,768,384]{2,1,0:T(8,128)(2,1)}, u32[]{:S(2)}, u32[]{:S(2)}) collective-permute-start(bf16[3,768,384]{2,1,0:T(8,128)(2,1)} %slice.497), channel_id=1, source_target_pairs={{0,1},{2,3},{4,5},{6,7},{8,9},{10,11},{12,13},{14,15},{16,17},{18,... | collective-permute-start | bytes 5308424 | tf_op jit(solution)/shard_map/ppermute | solution.py:10
  1131.0 138.4 %collective-permute-start.9 = (bf16[768,1536]{1,0:T(8,128)(2,1)}, bf16[768,1536]{1,0:T(8,128)(2,1)}, u32[]{:S(2)}, u32[]{:S(2)}) collective-permute-start(bf16[768,1536]{1,0:T(8,128)(2,1)} %slice.495), channel_id=1, source_target_pairs={{1,0},{3,2},{5,4},{7,6},{9,8},{11,10},{13,12},{15,14},{17,16},{19,... | collective-permute-start | bytes 7077896 | tf_op jit(solution)/shard_map/ppermute | solution.py:10
  1133.4 62.6 %collective-permute-start.7 = (bf16[384,768]{1,0:T(8,128)(2,1)S(1)}, bf16[384,768]{1,0:T(8,128)(2,1)}, u32[]{:S(2)}, u32[]{:S(2)}) collective-permute-start(bf16[384,768]{1,0:T(8,128)(2,1)S(1)} %slice.499), channel_id=1, source_target_pairs={{0,1},{2,3},{4,5},{6,7},{8,9},{10,11},{12,13},{14,15},{16,17},{18,... | collective-permute-start | bytes 1769480 | tf_op jit(solution)/shard_map/ppermute | solution.py:10
  1144.6 52.8 %copy-start.20 = (bf16[1,384,768]{2,1,0:T(8,128)(2,1)S(1)}, bf16[1,384,768]{2,1,0:T(8,128)(2,1)}, u32[]{:S(2)}) copy-start(bf16[1,384,768]{2,1,0:T(8,128)(2,1)} %fusion.370) | copy-start | bytes 1769476
  1148.3 386.3 %all-reduce.17.cloned.1.call-start = ((), (), s32[]{:S(2)}) async-start(), calls=%async_computation.4 | async-start | bytes 28311552 | tf_op jit(solution)/shard_map/psum | solution.py:273
  1148.3 53.3 %copy-start.12 = (bf16[1,3,768,384]{3,2,1,0:T(8,128)(2,1)S(1)}, bf16[1,3,768,384]{3,2,1,0:T(8,128)(2,1)}, u32[]{:S(2)}) copy-start(bf16[1,3,768,384]{3,2,1,0:T(8,128)(2,1)} %fusion.368) | copy-start | bytes 5308420
  1197.4 6.3 slice-start.10
  1198.6 5.2 slice-start.11
  1208.7 63.7 %copy-start.11 = (bf16[1,768,1536]{2,1,0:T(8,128)(2,1)S(1)}, bf16[1,768,1536]{2,1,0:T(8,128)(2,1)}, u32[]{:S(2)}) copy-start(bf16[1,768,1536]{2,1,0:T(8,128)(2,1)} %fusion.364) | copy-start | bytes 7077892
  1275.0 7.1 copy-start.56
  1275.0 7.1 copy-start.46
  1275.0 7.2 copy-start.45
  1275.0 8.5 copy-start.60
  1275.0 14.2 copy-start.5
  1275.0 14.2 copy-start.18
  1275.0 14.2 copy-start.25
  1275.0 14.2 copy-start.41
  1275.9 5.5 collective-permute-start.12
  1282.2 6.9 collective-permute-start.11
  1534.6 7.6 copy-start.13
  1542.1 4.5 copy-start.15
  (20 other events, 56.5 us)
Sparse Core Ops, SparseCore 0:
  287.7 121.5 all-reduce.8
  624.8 69.6 all-reduce.12
  697.6 211.0 all-reduce.10
  1148.4 120.8 all-reduce.14
  1275.2 259.3 all-reduce.16
where the time goes:
time: 1560 us
  waiting for transfers between devices  759 us (49%)
  matrix products  323 us (21%)
  other arithmetic  199 us (13%)
  local copies, waits for them, and re-layouts  110 us (7%)
  blocking collectives  67 us (4%)
  starting transfers between devices  52.7 us (3%)
  loops' own time  32.6 us (2%)
    psum x2, waiting for transfers between devices, body(): branch_total = lax.psum(partial_value, 'narrow')  302 us
    ppermute x15, waiting for transfers between devices, shifted_2(): return lax.ppermute(value, axis, pairs)  284 us
    psum x1, waiting for transfers between devices, body(): lax.psum(stacked[0].astype(jnp.bfloat16), 'wide').astype(jnp.float32)  172 us
    psum x1, blocking collectives, body(): lax.psum(stacked[5].astype(jnp.bfloat16), 'wide').astype(jnp.float32)  61.4 us
    sub x4, matrix products, attend(): shifted = jnp.exp(logits - jnp.max(logits, axis=-1, keepdims=True))  55.7 us
    ppermute x15, starting transfers between devices, shifted_2(): return lax.ppermute(value, axis, pairs)  52.5 us
    sub x2, matrix products, attend_back(): d_soft - row_dot  50.5 us
    dot_general x4, matrix products, attend(): jnp.einsum('bsd,kdhe->kbhse', normed_low, qkv_heads, preferred_element_ty...  39.6 us
  transfers between devices with their start and end apart: 20, of which 8 were waited for; matrix products, arithmetic and copies ran while one was open for 22% of the time, Pallas kernels for 0%

commit v1 on v0

--- a/solution.py
+++ b/solution.py
@@ -1,6 +1,10 @@
+import functools
+
 import jax
 import jax.numpy as jnp
 from jax import lax
+from jax.experimental import pallas as pl
+from jax.experimental.pallas import tpu as pltpu
 from jax.sharding import PartitionSpec as P
 
 
@@ -294,6 +298,530 @@
     )
 
 
+EPS = 1e-06
+F32 = jnp.float32
+BF16 = jnp.bfloat16
+GELU_IN = 0.7978845608028654
+GELU_CUBE = 0.044715
+
+
+def padded_to(length, step):
+    return -(-length // step) * step
+
+
+def dot(a, b):
+    return jnp.dot(a, b, preferred_element_type=F32)
+
+
+def dot_nt(a, b):
+    return lax.dot_general(a, b, (((1,), (1,)), ((), ())), preferred_element_type=F32)
+
+
+def normal_rows(x):
+    centered = x - jnp.mean(x, axis=-1, keepdims=True)
+    inverse = lax.rsqrt(jnp.mean(centered * centered, axis=-1, keepdims=True) + EPS)
+    return centered * inverse, inverse
+
+
+def back_rows(upstream, normal, inverse, gain):
+    scaled = upstream * gain
+    return inverse * (
+        scaled
+        - jnp.mean(scaled, axis=-1, keepdims=True)
+        - normal * jnp.mean(scaled * normal, axis=-1, keepdims=True)
+    )
+
+
+def live_of(count, rows):
+    return lax.broadcasted_iota(jnp.int32, (rows, 1), 0) < count
+
+
+def padded_rows(source, wide_rows, live):
+    slots = source.shape[0]
+    edge = slots // 8 * 8
+    wide_rows[edge:, :] = jnp.zeros((wide_rows.shape[0] - edge, wide_rows.shape[1]), F32)
+    wide_rows[:slots, :] = source[...].astype(F32)
+    return jnp.where(live, wide_rows[...], 0.0)
+
+
+def head_norm(x):
+    centered = x - jnp.mean(x, axis=0, keepdims=True)
+    inverse = lax.rsqrt(jnp.mean(centered * centered, axis=0, keepdims=True) + EPS)
+    return centered * inverse, inverse
+
+
+def head_back(upstream, normal, inverse, gain):
+    scaled = upstream * gain
+    return inverse * (
+        scaled
+        - jnp.mean(scaled, axis=0, keepdims=True)
+        - normal * jnp.mean(scaled * normal, axis=0, keepdims=True)
+    )
+
+
+def key_sizes(patch_ref, rows):
+    slot = lax.broadcasted_iota(jnp.int32, (rows, patch_ref.shape[-1]), 0)
+    named = jnp.where(patch_ref[0] == slot, 1.0, 0.0)
+    return jnp.sum(named, axis=-1, keepdims=True)
+
+
+def scores_of(proj, head, inner, gains, soft):
+    head_dim = gains.shape[0] // 2
+    at = head * head_dim
+    q_normal, q_inverse = head_norm(proj[at : at + head_dim, :])
+    k_normal, k_inverse = head_norm(proj[inner + at : inner + at + head_dim, :])
+    queries = (q_normal * gains[:head_dim, :]).astype(BF16).astype(F32) * head_dim ** (-0.5)
+    queries = queries.astype(BF16)
+    keys = (k_normal * gains[head_dim:, :]).astype(BF16)
+    values = proj[2 * inner + at : 2 * inner + at + head_dim, :].astype(BF16)
+    return q_normal, q_inverse, k_normal, k_inverse, queries, keys, values
+
+
+def soften(queries, keys, sizes, soft, rows):
+    scores = dot(keys.T[:rows], queries)
+    raised = jnp.exp(scores) * sizes
+    soft[:rows, :] = raised.astype(BF16)
+    return raised, 1.0 / jnp.sum(raised, axis=0, keepdims=True)
+
+
+def forward_kernel(first, rows, counts, tok, patch, gain, w_qkv, gains, w_out, w_up, b_up, w_down,
+                   out, wide_rows, normed, proj, soft, mixed):
+    step = pl.program_id(0)
+    inner = w_out.shape[0]
+    head_dim = gains.shape[0] // 2
+
+    @pl.when(step == 0)
+    def _():
+        normed[...] = jnp.zeros(normed.shape, BF16)
+        soft[...] = jnp.zeros(soft.shape, BF16)
+
+    live = live_of(counts[first + step], rows)
+    x = padded_rows(tok.at[0], wide_rows, live)
+    normed[:rows, :] = (normal_rows(x)[0] * gain[...]).astype(BF16)
+    for part in range(3):
+        proj[part * inner : (part + 1) * inner, :] = dot_nt(w_qkv[part], normed[...])
+    sizes = key_sizes(patch, rows)
+    for head in range(inner // head_dim):
+        at = head * head_dim
+        _, _, _, _, queries, keys, values = scores_of(proj, head, inner, gains, soft)
+        raised, over = soften(queries, keys, sizes, soft.at[head], rows)
+        mixed[at : at + head_dim, :] = (dot(values, soft[head]) * over).astype(BF16)
+    total = dot(mixed[...].T[:rows], w_out[...])
+    units = w_up.shape[1]
+    tile = units // 3
+    for at in range(0, units, tile):
+        pre = dot(normed[:rows, :], w_up[:, at : at + tile]) + b_up[:, at : at + tile]
+        hidden = 0.5 * pre * (1.0 + jnp.tanh(GELU_IN * (pre + GELU_CUBE * pre * pre * pre)))
+        total = total + dot(hidden.astype(BF16), w_down[at : at + tile, :])
+    out[...] = total.astype(BF16)
+
+
+def feed_kernel(top, first, rows, per_step, counts, *refs):
+    refs = list(refs)
+    tok, own, far, cot = refs[:4]
+    refs = refs[4:]
+    if not top:
+        own_grad, far_grad, gain_top = refs[:3]
+        refs = refs[3:]
+    gain, b_prev, w_up, b_up, w_down = refs[:5]
+    refs = refs[5:]
+    if top:
+        x_out, fed = refs[:2]
+        refs = refs[2:]
+    else:
+        g_out = refs[0]
+        refs = refs[1:]
+    normed, low, d_feed, hidden_out, d_pre_out, sum_up, sum_down, wide_rows = refs
+    step = pl.program_id(0)
+    slots = tok.shape[1]
+
+    @pl.when(step == 0)
+    def _():
+        sum_up[...] = jnp.zeros(sum_up.shape, F32)
+        sum_down[...] = jnp.zeros(sum_down.shape, F32)
+
+    for j in range(per_step):
+        block = slice(j * rows, (j + 1) * rows)
+        live = live_of(counts[first + step * per_step + j], rows)
+        x0 = padded_rows(tok.at[j], wide_rows, live)
+        branch = own[block, :].astype(F32) + far[block, :].astype(F32)
+        x1 = jnp.where(live, x0 + branch + b_prev[...], 0.0)
+        grad = padded_rows(cot.at[j], wide_rows, live)
+        if top:
+            x = x1
+            x_out[j] = x1[:slots]
+        else:
+            x = x0
+            normal, inverse = normal_rows(x1)
+            d_normed = own_grad[block, :].astype(F32) + far_grad[block, :].astype(F32)
+            grad = grad + back_rows(d_normed, normal, inverse, gain_top[...])
+            g_out[block, :] = grad
+        normed[block, :] = (normal_rows(x)[0] * gain[...]).astype(BF16)
+        low[block, :] = grad.astype(BF16)
+        sum_down[...] += jnp.sum(grad, axis=0, keepdims=True)
+    units = w_up.shape[1]
+    tile = units // 3
+    d_total = jnp.zeros((per_step * rows, tok.shape[2]), F32)
+    total = jnp.zeros((per_step * rows, tok.shape[2]), F32)
+    for at in range(0, units, tile):
+        part = slice(at, at + tile)
+        pre = dot(normed[...], w_up[:, part]) + b_up[:, part]
+        square = pre * pre
+        bent = jnp.tanh(pre * (GELU_IN + (GELU_IN * GELU_CUBE) * square))
+        half = 0.5 + 0.5 * bent
+        hidden = (pre * half).astype(BF16)
+        slope = half + (0.5 * pre) * (1.0 - bent * bent) * (GELU_IN + (3 * GELU_IN * GELU_CUBE) * square)
+        d_pre = (dot_nt(low[...], w_down[part, :]) * slope).astype(BF16)
+        hidden_out[:, part] = hidden
+        d_pre_out[:, part] = d_pre
+        sum_up[:, part] += jnp.sum(d_pre.astype(F32), axis=0, keepdims=True)
+        d_total = d_total + dot_nt(d_pre, w_up[:, part])
+        if top:
+            total = total + dot(hidden, w_down[part, :])
+    d_feed[...] = d_total.astype(BF16)
+    if top:
+        fed[...] = total.astype(BF16)
+
+
+def heads_kernel(top, rows, patch, normed_in, low_in, d_feed, *refs):
+    refs = list(refs)
+    if top:
+        fed = refs[0]
+        refs = refs[1:]
+    w_qkv, gains, w_out = refs[:3]
+    refs = refs[3:]
+    if top:
+        out = refs[0]
+        refs = refs[1:]
+    d_normed, mixed_out, d_q, d_k, d_v, sum_gain, sum_row = refs[:7]
+    normed, low, proj, d_mixed, soft, d_soft, mixed, d_proj = refs[7:]
+    step = pl.program_id(0)
+    inner = w_out.shape[0]
+    head_dim = gains.shape[0] // 2
+
+    @pl.when(step == 0)
+    def _():
+        normed[...] = jnp.zeros(normed.shape, BF16)
+        low[...] = jnp.zeros(low.shape, BF16)
+        soft[...] = jnp.zeros(soft.shape, BF16)
+        d_soft[...] = jnp.zeros(d_soft.shape, BF16)
+        sum_gain[...] = jnp.zeros(sum_gain.shape, F32)
+        sum_row[...] = jnp.zeros(sum_row.shape, F32)
+
+    normed[:rows, :] = normed_in[...]
+    low[:rows, :] = low_in[...]
+    for part in range(3):
+        proj[part * inner : (part + 1) * inner, :] = dot_nt(w_qkv[part], normed[...])
+    d_mixed[...] = dot_nt(w_out[...], low[...]).astype(BF16)
+    sizes = key_sizes(patch, rows)
+    q_gain, k_gain = gains[:head_dim, :], gains[head_dim:, :]
+    for head in range(inner // head_dim):
+        at = head * head_dim
+        here = slice(at, at + head_dim)
+        q_normal, q_inverse, k_normal, k_inverse, queries, keys, values = scores_of(proj, head, inner, gains, soft)
+        raised, over = soften(queries, keys, sizes, soft.at[head], rows)
+        mixed_here = dot(values, soft[head]) * over
+        mixed[here, :] = mixed_here.astype(BF16)
+        d_mixed_here = d_mixed[here, :].astype(F32)
+        row_dot = jnp.sum(d_mixed_here * mixed_here, axis=0, keepdims=True) * over
+        scaled = (d_mixed_here * over).astype(BF16)
+        slope = dot(values.T[:rows], scaled)
+        d_soft[head, :rows, :] = (raised * (slope - row_dot)).astype(BF16)
+        d_queries = dot(keys, d_soft[head]) * head_dim ** (-0.5)
+        d_keys = dot_nt(queries, d_soft[head])
+        sum_gain[:head_dim, :] += d_queries * q_normal
+        sum_gain[head_dim:, :] += d_keys * k_normal
+        d_proj[here, :] = head_back(d_queries, q_normal, q_inverse, q_gain).astype(BF16)
+        d_proj[inner + at : inner + at + head_dim, :] = head_back(d_keys, k_normal, k_inverse, k_gain).astype(BF16)
+        d_proj[2 * inner + at : 2 * inner + at + head_dim, :] = dot_nt(scaled, soft[head]).astype(BF16)
+    mixed_rows = mixed[...].T[:rows]
+    mixed_out[...] = mixed_rows
+    if top:
+        out[...] = (fed[...].astype(F32) + dot(mixed_rows, w_out[...])).astype(BF16)
+    total = d_feed[...].astype(F32)
+    for part, target in enumerate((d_q, d_k, d_v)):
+        d_rows = d_proj[part * inner : (part + 1) * inner, :].T[:rows]
+        target[...] = d_rows
+        total = total + dot(d_rows, w_qkv[part])
+    d_normed[...] = total.astype(BF16)
+    sum_row[...] += jnp.sum(total * normed_in[...].astype(F32), axis=0, keepdims=True)
+
+
+def second_kernel(rows, counts, tok, own, far, own_next, far_next, b_first, b_next, out, wide_rows):
+    slots = tok.shape[1]
+    live = live_of(counts[pl.program_id(0)], rows)
+    x0 = padded_rows(tok.at[0], wide_rows, live)
+    x1 = jnp.where(live, x0 + (own[...].astype(F32) + far[...].astype(F32)) + b_first[...], 0.0)
+    branch = own_next[...].astype(F32) + far_next[...].astype(F32)
+    out[0] = jnp.where(live, x1 + branch + b_next[...], 0.0)[:slots]
+
+
+def tokens_kernel(rows, counts, tok, grad, own, far, gain, out, wide_rows):
+    slots = tok.shape[1]
+    live = live_of(counts[pl.program_id(0)], rows)
+    normal, inverse = normal_rows(padded_rows(tok.at[0], wide_rows, live))
+    d_normed = own[...].astype(F32) + far[...].astype(F32)
+    out[0] = (grad[...] + back_rows(d_normed, normal, inverse, gain[...]))[:slots]
+
+
+def whole_spec(array):
+    return pl.BlockSpec(array.shape, lambda i, *_: (0,) * array.ndim)
+
+
+def rows_spec(rows, columns, first=0):
+    return pl.BlockSpec((rows, columns), lambda i, *_: (first + i, 0))
+
+
+def image_spec(images, slots, columns, first=0):
+    return pl.BlockSpec((images, slots, columns), lambda i, *_: (first + i, 0, 0))
+
+
+def params(mib):
+    return pltpu.CompilerParams(dimension_semantics=("arbitrary",), vmem_limit_bytes=mib * 1024 * 1024)
+
+
+def cost(flops, moved):
+    return pl.CostEstimate(flops=flops, bytes_accessed=moved, transcendentals=0)
+
+
+def split_body(tokens, merge_map, counts, ln_gain, w_qkv, qk_gain, w_out, w_up, b_up, w_down, b_down, cotangent):
+    images, slots, dim = tokens.shape
+    layers, inner = w_out.shape[:2]
+    units = w_up.shape[2]
+    head_dim = qk_gain.shape[-1]
+    heads = inner // head_dim
+    rows, lanes = padded_to(slots, 16), padded_to(slots, 128)
+    n_narrow = lax.axis_size("narrow")
+    all_rows = images * rows
+
+    def others(value):
+        if n_narrow == 2:
+            return lax.ppermute(value, "narrow", [(0, 1), (1, 0)])
+        wide_value = value.astype(F32)
+        return (lax.psum(wide_value, "narrow") - wide_value).astype(BF16)
+
+    patches = jnp.pad(merge_map, ((0, 0), (0, lanes - slots)), constant_values=-1)[:, None, :]
+    turned = jnp.swapaxes(w_qkv, 2, 3)
+    gains = qk_gain.reshape(layers, 2 * head_dim, 1)
+    bias_up = b_up.astype(F32)[:, None, :]
+    ln = ln_gain[:, None, :]
+    bias_down = b_down[:, None, :]
+    row_array = jax.ShapeDtypeStruct((all_rows, dim), BF16)
+    unit_array = jax.ShapeDtypeStruct((all_rows, units), BF16)
+    head_array = jax.ShapeDtypeStruct((all_rows, inner), BF16)
+    image_array = jax.ShapeDtypeStruct((images, slots, dim), F32)
+    head_flops = 2 * all_rows * dim * inner * 4 + 4 * all_rows * rows * inner
+    feed_flops = 2 * all_rows * dim * units * 2
+    layer_bytes = 2 * (4 * dim * inner + 2 * dim * units)
+
+    def call(kernel, operands, specs, shapes, out_specs, scratch, grid, flops, moved, mib, prefetch=1):
+        return pl.pallas_call(
+            kernel,
+            grid_spec=pltpu.PrefetchScalarGridSpec(
+                num_scalar_prefetch=prefetch,
+                grid=(grid,),
+                in_specs=specs,
+                out_specs=out_specs,
+                scratch_shapes=scratch,
+            ),
+            out_shape=shapes,
+            compiler_params=params(mib),
+            cost_estimate=cost(flops, moved),
+        )(*operands)
+
+    wide_rows = pltpu.VMEM((rows, dim), F32)
+    head_scratch = [
+        pltpu.VMEM((lanes, dim), BF16),
+        pltpu.VMEM((3 * inner, lanes), F32),
+        pltpu.VMEM((heads, lanes, lanes), BF16),
+        pltpu.VMEM((inner, lanes), BF16),
+    ]
+    tok_spec = image_spec(1, slots, dim)
+    patch_spec = image_spec(1, 1, lanes)
+    row_spec = rows_spec(rows, dim)
+
+    def forward(layer):
+        weights = (ln[layer], turned[layer], gains[layer], w_out[layer], w_up[layer], bias_up[layer], w_down[layer])
+        return call(
+            functools.partial(forward_kernel, 0, rows),
+            (counts, tokens, patches) + weights,
+            [tok_spec, patch_spec] + [whole_spec(w) for w in weights],
+            row_array,
+            row_spec,
+            [wide_rows] + head_scratch,
+            images,
+            head_flops + feed_flops,
+            layer_bytes,
+            40,
+        )
+
+    def feed_back(layer, top, pieces):
+        per_step = 2
+        weights = (ln[layer], bias_down[0], w_up[layer], bias_up[layer], w_down[layer])
+        if not top:
+            weights = (ln[layer + 1],) + weights
+        block = per_step * rows
+        extra = [image_array, row_array] if top else [jax.ShapeDtypeStruct((all_rows, dim), F32)]
+        extra_specs = [image_spec(per_step, slots, dim), rows_spec(block, dim)] if top else [rows_spec(block, dim)]
+        outs = extra + [
+            row_array,
+            row_array,
+            row_array,
+            unit_array,
+            unit_array,
+            jax.ShapeDtypeStruct((1, units), F32),
+            jax.ShapeDtypeStruct((1, dim), F32),
+        ]
+        out_specs = extra_specs + [
+            rows_spec(block, dim),
+            rows_spec(block, dim),
+            rows_spec(block, dim),
+            rows_spec(block, units),
+            rows_spec(block, units),
+            whole_spec(outs[-2]),
+            whole_spec(outs[-1]),
+        ]
+        operands = (tokens, pieces[0], pieces[1], cotangent) + tuple(pieces[2:])
+        image_block = image_spec(per_step, slots, dim)
+        specs = [image_block, rows_spec(block, dim), rows_spec(block, dim), image_block]
+        specs += [rows_spec(block, dim)] * len(pieces[2:])
+        return call(
+            functools.partial(feed_kernel, top, 0, rows, per_step),
+            (counts,) + operands + weights,
+            specs + [whole_spec(w) for w in weights],
+            outs,
+            out_specs,
+            [wide_rows],
+            images // per_step,
+            2 * feed_flops,
+            layer_bytes * 2 + 12 * all_rows * dim * 2,
+            56,
+        )
+
+    def heads_back(layer, top, normed, low, d_feed, fed):
+        weights = (turned[layer], gains[layer], w_out[layer])
+        streams = (normed, low, d_feed) + ((fed,) if top else ())
+        outs = ([row_array] if top else []) + [
+            row_array,
+            head_array,
+            head_array,
+            head_array,
+            head_array,
+            jax.ShapeDtypeStruct((2 * head_dim, lanes), F32),
+            jax.ShapeDtypeStruct((1, dim), F32),
+        ]
+        out_specs = ([row_spec] if top else []) + [
+            row_spec,
+            rows_spec(rows, inner),
+            rows_spec(rows, inner),
+            rows_spec(rows, inner),
+            rows_spec(rows, inner),
+            whole_spec(outs[-2]),
+            whole_spec(outs[-1]),
+        ]
+        return call(
+            functools.partial(heads_kernel, top, rows),
+            (patches,) + streams + weights,
+            [patch_spec] + [row_spec] * len(streams) + [whole_spec(w) for w in weights],
+            outs,
+            out_specs,
+            [head_scratch[0]] * 2
+            + [head_scratch[1], head_scratch[3], head_scratch[2], head_scratch[2], head_scratch[3]]
+            + [pltpu.VMEM((3 * inner, lanes), BF16)],
+            images,
+            3 * head_flops,
+            layer_bytes * 2,
+            40,
+            prefetch=0,
+        )
+
+    def weight_grad(left, right):
+        return lax.dot_general(left, right, (((0,), (0,)), ((), ())), preferred_element_type=F32).astype(BF16)
+
+    own = forward(0)
+    far = others(own)
+    first_out, fed, normed, low, d_feed, hidden, d_pre, s_up1, s_down1 = feed_back(1, True, (own, far))
+    up1, down1 = lax.psum((weight_grad(normed, d_pre), weight_grad(hidden, low)), "wide")
+    own_next, own_grad, mixed, d_q, d_k, d_v, s_gain1, s_row1 = heads_back(1, True, normed, low, d_feed, fed)
+    far_grad = others(own_grad)
+    far_next = others(own_next)
+    qkv1 = [weight_grad(normed, part) for part in (d_q, d_k, d_v)]
+    qkv1, out1 = lax.psum((qkv1, weight_grad(mixed, low)), "wide")
+    g_first, normed, low, d_feed, hidden, d_pre, s_up0, s_down0 = feed_back(
+        0, False, (own, far, own_grad, far_grad)
+    )
+    up0, down0 = lax.psum((weight_grad(normed, d_pre), weight_grad(hidden, low)), "wide")
+    own_grad, mixed, d_q, d_k, d_v, s_gain0, s_row0 = heads_back(0, False, normed, low, d_feed, None)
+    far_grad = others(own_grad)
+    qkv0 = [weight_grad(normed, part) for part in (d_q, d_k, d_v)]
+    qkv0, out0 = lax.psum((qkv0, weight_grad(mixed, low)), "wide")
+    second_out = call(
+        functools.partial(second_kernel, rows),
+        (counts, tokens, own, far, own_next, far_next, bias_down[0], bias_down[1]),
+        [tok_spec] + [row_spec] * 4 + [whole_spec(bias_down[0])] * 2,
+        image_array,
+        tok_spec,
+        [wide_rows],
+        images,
+        10 * all_rows * dim,
+        12 * all_rows * dim,
+        16,
+    )
+    grad_tokens = call(
+        functools.partial(tokens_kernel, rows),
+        (counts, tokens, g_first, own_grad, far_grad, ln[0]),
+        [tok_spec] + [row_spec] * 3 + [whole_spec(ln[0])],
+        image_array,
+        tok_spec,
+        [wide_rows],
+        images,
+        10 * all_rows * dim,
+        12 * all_rows * dim,
+        16,
+    )
+    here = lax.axis_index("narrow")
+    up_sums = jnp.concatenate([s_up0, s_up1])
+    placed = jnp.where(jnp.arange(n_narrow)[None, :, None] == here, up_sums[:, None, :], 0.0)
+    small = jnp.concatenate(
+        [
+            jnp.concatenate([s_row0, s_row1]) / ln_gain,
+            jnp.sum(jnp.stack([s_gain0, s_gain1]), axis=-1),
+            jnp.concatenate([s_down0, s_down1]) / n_narrow,
+            placed.reshape(layers, n_narrow * units),
+        ],
+        axis=1,
+    )
+    small = lax.psum(small, ("wide", "narrow"))
+    g_ln = small[:, :dim]
+    g_gain = small[:, dim : dim + 2 * head_dim].reshape(qk_gain.shape)
+    g_b_down = small[:, dim + 2 * head_dim : 2 * dim + 2 * head_dim]
+    g_b_up = small[:, 2 * dim + 2 * head_dim :].reshape(layers, n_narrow, units)
+    g_b_up = lax.dynamic_index_in_dim(g_b_up, here, axis=1, keepdims=False)
+
+    def both(lower, upper):
+        return jnp.stack([lower, upper]).astype(F32)
+
+    return (
+        first_out,
+        second_out,
+        grad_tokens,
+        g_ln,
+        jnp.stack([jnp.stack(qkv0), jnp.stack(qkv1)]).astype(F32),
+        g_gain,
+        both(out0, out1),
+        both(up0, up1),
+        g_b_up,
+        both(down0, down1),
+        g_b_down,
+    )
+
+
+def pick_body(*arrays):
+    if arrays[4].shape[-1] % arrays[5].shape[-1] == 0:
+        return split_body(*arrays)
+    return body(*arrays)
+
+
 def solution(mesh):
     placed = (
         P("wide", None, None),
@@ -310,7 +838,7 @@
         P("wide", None, None),
     )
     return jax.shard_map(
-        body,
+        pick_body,
         mesh=mesh,
         in_specs=placed,
         out_specs=(

time: 1560 us -> 642 us (0.41)
  waiting for transfers between devices: 759 us -> 182 us
  matrix products: 323 us -> 46.2 us
  other arithmetic: 199 us -> 16.7 us
  Pallas kernels: 0 us -> 176 us
  blocking collectives: 67 us -> 138 us
  local copies, waits for them, and re-layouts: 110 us -> 53.8 us
  starting transfers between devices: 52.7 us -> 6.59 us
  loops' own time: 32.6 us -> 0 us
    psum x5 -> x1, waiting for transfers between devices: 475 us -> 92.1 us  [split_body(): qkv1, out1 = lax.psum((qkv1, weight_grad(mixed, low)), 'wide')]
    ppermute x15 -> x4, waiting for transfers between devices: 284 us -> 89.6 us  [others(): return lax.ppermute(value, 'narrow', [(0, 1), (1, 0)])]
    pallas_call x0 -> x7, Pallas kernels: none -> 176 us  [call(): pl.pallas_call(kernel, grid_spec=pltpu.PrefetchScalarGridSpec(num_scalar_...]
    dot_general x20 -> x12, matrix products: 217 us -> 46.2 us  [weight_grad(): lax.dot_general(left, right, (((0,), (0,)), ((), ())), preferred_element_...]
    sub x6 -> x0, matrix products: 106 us -> none  [the longest x4 55.7 us: attend(): shifted = jnp.exp(logits - jnp.max(logits, axis=-1, keepdims=True))]
    psum x2 -> x1, blocking collectives: 67 us -> 138 us  [split_body(): small = lax.psum(small, ('wide', 'narrow'))]
    another operation x22 -> x1, other arithmetic: 59.3 us -> 0.54 us  [split_body(): jnp.stack([jnp.stack(qkv0), jnp.stack(qkv1)]).astype(F32)]
    convert_element_type x17 -> x4, other arithmetic: 71.9 us -> 15.9 us  [the longest x3 12 us: both(): return jnp.stack([lower, upper]).astype(F32)]
  transfers between devices with their start and end apart: 20 -> 5, of which waited for: 8 -> 3; matrix products, arithmetic and copies ran while one was open for 22% -> 6% of each run, Pallas kernels for 0% -> 2%
where the time goes in v1:
time: 642 us; the launch traced here: 634 us
  waiting for transfers between devices  182 us (28%)
  Pallas kernels  176 us (27%)
  blocking collectives  138 us (21%)
  local copies, waits for them, and re-layouts  53.8 us (8%)
  matrix products  46.2 us (7%)
  other arithmetic  16.7 us (3%)
  between operations  14.9 us (2%)
  starting transfers between devices  6.59 us (1%)
    pallas_call x7, Pallas kernels, call(): pl.pallas_call(kernel, grid_spec=pltpu.PrefetchScalarGridSpec(num_scalar_...  176 us
    psum x1, blocking collectives, split_body(): small = lax.psum(small, ('wide', 'narrow'))  138 us
    psum x1, waiting for transfers between devices, split_body(): qkv1, out1 = lax.psum((qkv1, weight_grad(mixed, low)), 'wide')  92.1 us
    ppermute x4, waiting for transfers between devices, others(): return lax.ppermute(value, 'narrow', [(0, 1), (1, 0)])  89.6 us
    dot_general x12, matrix products, weight_grad(): lax.dot_general(left, right, (((0,), (0,)), ((), ())), preferred_element_...  46.2 us
    unnamed x103, local copies, waits for them, and re-layouts  34.9 us
  transfers between devices with their start and end apart: 5, of which 3 were waited for; matrix products, arithmetic and copies ran while one was open for 6% of the time, Pallas kernels for 2%

profile of v1, /device:TPU:0, one launch (start us, length us, event | category | flops | bytes accessed | tf_op | source)
XLA Modules:
  0.0 633.6 jit_solution(17361680746179409672)
XLA Ops:
  7.2 0.0 all-reduce.4.cloned.1.call-start
  7.2 0.7 fusion.16
  7.9 1.3 fusion.15
  9.3 0.7 pad.4
  10.0 1.4 fusion.14
  11.4 0.1 squeeze.63.gains.refs_1_
  11.5 2.2 slice_bitcast_fusion.6
  13.7 2.1 copy.26.tok.refs_0_
  15.8 6.3 copy.23
  22.1 3.6 slice_bitcast_fusion.4
  25.8 4.7 slice_bitcast_fusion.1
  30.5 1.9 slice_bitcast_fusion
  32.5 0.2 copy-done.5
  32.7 31.8 %shard_map.203.refs_1_.own = bf16[1664,768]{1,0:T(8,128)(2,1)} custom-call(s32[8]{0:T(128)S(1)} %copy-done.15, bf16[8,196,768]{2,1,0:T(8,128)(2,1)S(1)} %copy.26.tok.refs_0_, s32[8,1,256]{2,1,0:T(1,128)S(1)} %broadcast_in_dim.34.patch, f32[1,768]{1,0:T(1,128)S(1)} %get-tuple-element.113.gain.refs_7_, ...), custom_call_target="tpu_custom_call" | custom-call | flops 12309233664 | bytes 7077888 | tf_op jit(solution)/shard_map/pallas_call | solution.py:618
  64.5 3.0 collective-permute-start
  67.4 0.1 squeeze.62.refs_2_
  67.6 3.6 copy.27.refs_3_
  71.2 0.6 fusion.13
  71.8 51.3 %collective-permute-done.refs_2_.far = bf16[1664,768]{1,0:T(8,128)(2,1)S(1)} collective-permute-done((bf16[1664,768]{1,0:T(8,128)(2,1)}, bf16[1664,768]{1,0:T(8,128)(2,1)S(1)}, u32[]{:S(2)}, u32[]{:S(2)}) %collective-permute-start) | collective-permute-done | bytes 2555936 | tf_op jit(solution)/shard_map/ppermute | solution.py:599
  123.1 1.5 copy-done.3
  124.6 28.5 %shard_map.204 = (f32[8,196,768]{2,1,0:T(8,128)}, bf16[1664,768]{1,0:T(8,128)(2,1)}, bf16[1664,768]{1,0:T(8,128)(2,1)}, bf16[1664,768]{1,0:T(8,128)(2,1)}, bf16[...) custom-call(s32[8]{0:T(128)} %counts.9, ...), custom_call_target="tpu_custom_call" | custom-call | flops 15703474176 | bytes 44826624 | tf_op jit(solution)/shard_map/pallas_call | solution.py:618
  153.1 0.0 copy-start.39
  153.1 37.4 %shard_map.205 = (bf16[1664,768]{1,0:T(8,128)(2,1)}, bf16[1664,768]{1,0:T(8,128)(2,1)S(1)}, bf16[1664,384]{1,0:T(8,128)(2,1)S(1)}, bf16[1664,384]{1,0:T(8,128)(2...) custom-call(s32[8,1,256]{2,1,0:T(1,128)S(1)} %broadcast_in_dim.34.pa, ...), custom_call_target="tpu_custom_call" | custom-call | flops 13372489728 | bytes 14155776 | tf_op jit(solution)/shard_map/pallas_call | solution.py:618
  190.6 2.4 fusion.7
  193.0 2.4 fusion.8
  195.4 1.8 collective-permute-start.2
  197.2 2.1 fusion.11
  199.3 2.4 fusion.9
  201.7 5.9 fusion.1
  207.6 6.1 fusion.3
  213.8 38.3 %collective-permute-done.2.refs_5_ = bf16[1664,768]{1,0:T(8,128)(2,1)S(1)} collective-permute-done((bf16[1664,768]{1,0:T(8,128)(2,1)S(1)}, bf16[1664,768]{1,0:T(8,128)(2,1)S(1)}, u32[]{:S(2)}, u32[]{:S(2)}) %collective-permute-start.2) | collective-permute-done | bytes 2555936 | tf_op jit(solution)/shard_map/ppermute | solution.py:599
  252.0 1.5 copy-done.35
  253.5 27.4 %shard_map.207 = (f32[1664,768]{1,0:T(8,128)}, bf16[1664,768]{1,0:T(8,128)(2,1)}, bf16[1664,768]{1,0:T(8,128)(2,1)}, bf16[1664,768]{1,0:T(8,128)(2,1)}, bf16[166...) custom-call(s32[8]{0:T(128)} %counts.9, bf16[8,196,768]{2,1,0:T(8,128)(2,1)} %copy-done, ...), custom_call_target="tpu_custom_call" | custom-call | flops 15703474176 | bytes 44826624 | tf_op jit(solution)/shard_map/pallas_call | solution.py:618
  280.9 0.0 copy-start.40
  281.0 9.3 %fusion = bf16[1,768,1536]{2,1,0:T(8,128)(2,1)} fusion(bf16[1664,768]{1,0:T(8,128)(2,1)} %get-tuple-element.51.normed_in, bf16[1664,1536]{1,0:T(8,128)(2,1)} %get-tuple-element.71), kind=kOutput, calls=%fused_computation.7 | convolution fusion | flops 3927048192 | bytes 10027008 | tf_op jit(solution)/shard_map/dot_general | solution.py:739
  290.3 6.1 fusion.2
  296.4 35.2 %shard_map.208 = (bf16[1664,768]{1,0:T(8,128)(2,1)}, bf16[1664,384]{1,0:T(8,128)(2,1)S(1)}, bf16[1664,384]{1,0:T(8,128)(2,1)S(1)}, bf16[1664,384]{1,0:T(8,128)(2...) custom-call(s32[8,1,256]{2,1,0:T(1,128)S(1)} %broadcast_in_dim.34.patch, ...), custom_call_target="tpu_custom_call" | custom-call | flops 13372489728 | bytes 14155776 | tf_op jit(solution)/shard_map/pallas_call | solution.py:618
  331.6 2.1 fusion.10
  333.7 2.4 fusion.4
  336.1 2.4 fusion.5
  338.5 2.4 fusion.6
  340.9 0.0 all-reduce.4.cloned.1.call-update
  340.9 1.5 collective-permute-start.1
  342.4 0.1 broadcast_in_dim.35
  342.6 6.6 %copy.34 = f32[8,196,768]{2,0,1:T(8,128)} copy(f32[8,196,768]{2,1,0:T(8,128)} %get-tuple-element.75) | data formatting | bytes 9633792
  349.2 0.3 collective-permute-start.3
  349.6 0.1 maximum_reduce_fusion
  349.8 138.0 %psum.91 = f32[2,4736]{1,0:T(2,128)S(1)} all-reduce(f32[2,4736]{1,0:T(2,128)S(1)} %pad_maximum_fusion), channel_id=1, replica_groups=mesh['wide'=16,'narrow'=2] {'wide','narrow'}, use_global_device_ids=true, to_apply=%region_1.2 | all-reduce | flops 9472 | bytes 75776 | tf_op jit(solution)/shard_map/psum | solution.py:794
  487.9 1.7 copy-done.4
  489.6 8.0 %shard_map.206 = f32[8,196,768]{2,1,0:T(8,128)S(1)} custom-call(s32[8]{0:T(128)S(1)} %copy-done.16, bf16[8,196,768]{2,1,0:T(8,128)(2,1)S(1)} %copy-done.1, bf16[1664,768]{1,0:T(8,128)(2,1)} %shard_map.203.refs_1_.own, bf16[1664,768]{1,0:T(8,128)(2,1)S(1)} %copy-done.4, bf16[1664,768]{1,0:T(8,128)(2,1)} %get-tuple-element.48.own_next, ...), custom_call_target="tpu_custom_call" | custom-call | flops 12779520 | bytes 15335424 | tf_op jit(solution)/shard_map/pallas_call | solution.py:618
  497.6 3.7 copy.35
  501.3 0.7 reshape.54
  502.0 0.6 copy.40
  502.6 0.6 fusion.12
  503.3 2.4 copy-done.2
  505.7 7.5 %shard_map.209 = f32[8,196,768]{2,1,0:T(8,128)S(1)} custom-call(s32[8]{0:T(128)S(1)} %copy-done.16, bf16[8,196,768]{2,1,0:T(8,128)(2,1)S(1)} %copy-done.1, f32[1664,768]{1,0:T(8,128)S(1)} %copy-done.2, bf16[1664,768]{1,0:T(8,128)(2,1)} %get-tuple-element.54.own, bf16[1664,768]{1,0:T(8,128)(2,1)} %collective-permute-done.3.far, f32[1,768]{1,0:T(1,128)S(1)} %copy-done.13), custom_call_target="tpu_custom_call" | custom-call | flops 12779520 | bytes 15335424 | tf_op jit(solution)/shard_map/pallas_call | solution.py:618
  513.2 3.7 copy.36
  516.9 92.1 %all-reduce.4.cloned.1.call-done = (bf16[1,768,384]{2,1,0:T(8,128)(2,1)}, bf16[1,768,384]{2,1,0:T(8,128)(2,1)}, bf16[1,768,384]{2,1,0:T(8,128)(2,1)}, bf16[1,768...) async-done(((bf16[1,768,384]{2,1,0:T(8,128)(2,1)}, ...) | async-done | bytes 14155792 | tf_op jit(solution)/shard_map/psum | solution.py:749
  609.0 3.0 maximum_convert_fusion.3
  612.0 0.5 maximum_bitcast_fusion
  612.6 3.9 maximum_convert_fusion.2
  616.5 0.7 copy-done.22
  617.2 4.7 maximum_convert_fusion
  621.9 4.4 maximum_convert_fusion.1
  (104 shorter events, 0.4 us)
Async XLA Ops:
  7.2 601.8 %all-reduce.4.cloned.1.call-start = ((), (), s32[]{:S(2)}) async-start(), calls=%async_computation | async-start | bytes 28311552 | tf_op jit(solution)/shard_map/psum | solution.py:749
  9.3 23.2 %copy-start.12 = (f32[1,768]{1,0:T(1,128)}, f32[1,768]{1,0:T(1,128)S(1)}, u32[]{:S(2)}) copy-start(f32[1,768]{1,0:T(1,128)S(1)} %get-tuple-element.113.gain.refs_7_) | copy-start | bytes 9220
  11.4 21.1 %copy-start.14 = (f32[1,1536]{1,0:T(1,128)}, f32[1,1536]{1,0:T(1,128)S(1)}, u32[]{:S(2)}) copy-start(f32[1,1536]{1,0:T(1,128)S(1)} %get-tuple-element.111.b_up.refs_10_) | copy-start | bytes 18436
  15.8 16.7 %copy-start = (bf16[8,196,768]{2,1,0:T(8,128)(2,1)}, bf16[8,196,768]{2,1,0:T(8,128)(2,1)S(1)}, u32[]{:S(2)}) copy-start(bf16[8,196,768]{2,1,0:T(8,128)(2,1)S(1)} %copy.26.tok.refs_0_) | copy-start | bytes 7225348
  22.1 8.4 %slice-start = ((s8[4718592]{0:T(1024)(128)(4,1)}), s8[4194304]{0:T(1024)(128)(4,1)S(1)}, s32[]{:S(2)}) async-start(s8[4718592]{0:T(1024)(128)(4,1)} %bitcast.80), calls=%async_computation.1 | async-start | bytes 8388608
  25.8 6.7 %copy-start.7 = (bf16[3,384,768]{2,1,0:T(8,128)(2,1)}, bf16[3,384,768]{2,1,0:T(8,128)(2,1)S(1)}, u32[]{:S(2)}) copy-start(bf16[3,384,768]{2,1,0:T(8,128)(2,1)S(1)} %get-tuple-element.103.w_qkv.refs_0_) | copy-start | bytes 5308420
  25.8 4.8 slice-start.1
  30.5 2.2 copy-start.5
  30.5 2.2 copy-start.15
  32.5 32.0 %copy-start.6 = (bf16[1536,768]{1,0:T(8,128)(2,1)}, bf16[1536,768]{1,0:T(8,128)(2,1)S(1)}, u32[]{:S(2)}) copy-start(bf16[1536,768]{1,0:T(8,128)(2,1)S(1)} %get-tuple-element.99.w_down.refs_11_) | copy-start | bytes 7077892
  64.5 6.7 %copy-start.30 = (f32[2,768]{1,0:T(2,128)S(1)}, f32[2,768]{1,0:T(2,128)}, u32[]{:S(2)}) copy-start(f32[2,768]{1,0:T(2,128)} %param.22) | copy-start | bytes 18436
  64.5 58.6 %collective-permute-start = (bf16[1664,768]{1,0:T(8,128)(2,1)}, bf16[1664,768]{1,0:T(8,128)(2,1)S(1)}, u32[]{:S(2)}, u32[]{:S(2)}) collective-permute-start(bf16[1664,768]{1,0:T(8,128)(2,1)} %shard_map.203.refs_1_.own), channel_id=1, source_target_pairs={{0,1},{1,0},{2,3},{3,2},{4,5},{5,4},{6,7},{7,6},{8,9},{9,8},{10,11... | collective-permute-start | bytes 7667720 | tf_op jit(solution)/shard_map/ppermute | solution.py:599
  123.1 1.5 copy-start.3
  124.6 28.5 %copy-start.9 = (bf16[3,384,768]{2,1,0:T(8,128)(2,1)S(1)}, bf16[3,384,768]{2,1,0:T(8,128)(2,1)}, u32[]{:S(2)}) copy-start(bf16[3,384,768]{2,1,0:T(8,128)(2,1)} %get-tuple-element.102.refs_1_) | copy-start | bytes 5308420
  124.6 28.5 %copy-start.10 = (bf16[384,768]{1,0:T(8,128)(2,1)S(1)}, bf16[384,768]{1,0:T(8,128)(2,1)}, u32[]{:S(2)}) copy-start(bf16[384,768]{1,0:T(8,128)(2,1)} %get-tuple-element.104.refs_3_) | copy-start | bytes 1769476
  153.1 37.4 %copy-start.39 = (bf16[1664,768]{1,0:T(8,128)(2,1)S(1)}, bf16[1664,768]{1,0:T(8,128)(2,1)}, u32[]{:S(2)}) copy-start(bf16[1664,768]{1,0:T(8,128)(2,1)} %get-tuple-element.44.normed_in) | copy-start | bytes 7667716
  190.6 4.8 copy-start.17
  193.0 4.2 copy-start.36
  193.0 8.7 %slice-start.2 = ((s8[5111808]{0:T(1024)(128)(4,1)}), s8[4194304]{0:T(1024)(128)(4,1)S(1)}, s32[]{:S(2)}) async-start(s8[5111808]{0:T(1024)(128)(4,1)} %bitcast.84), calls=%async_computation.3 | async-start | bytes 8388608
  195.4 56.7 %collective-permute-start.2 = (bf16[1664,768]{1,0:T(8,128)(2,1)S(1)}, bf16[1664,768]{1,0:T(8,128)(2,1)S(1)}, u32[]{:S(2)}, u32[]{:S(2)}) collective-permute-start(bf16[1664,768]{1,0:T(8,128)(2,1)S(1)} %get-tuple-element.49.refs_4_), channel_id=1, source_target_pairs={{0,1},{1,0},{2,3},{3,2},{4,5},{5,4},{6,7},{7,6},{8,9},{9,8},{10,11... | collective-permute-start | bytes 7667720 | tf_op jit(solution)/shard_map/ppermute | solution.py:599
  197.2 4.6 slice-start.3
  199.3 8.3 %slice-start.4 = ((s8[5111808]{0:T(1024)(128)(4,1)}), s8[4194304]{0:T(1024)(128)(4,1)S(1)}, s32[]{:S(2)}) async-start(s8[5111808]{0:T(1024)(128)(4,1)} %bitcast.86), calls=%async_computation.5 | async-start | bytes 8388608
  201.7 5.9 slice-start.5
  252.0 1.5 copy-start.35
  280.9 9.3 %copy-start.37 = (bf16[1664,768]{1,0:T(8,128)(2,1)S(1)}, bf16[1664,768]{1,0:T(8,128)(2,1)}, u32[]{:S(2)}) copy-start(bf16[1664,768]{1,0:T(8,128)(2,1)} %get-tuple-element.52.low_in) | copy-start | bytes 7667716
  280.9 9.3 %copy-start.40 = (bf16[1664,1536]{1,0:T(8,128)(2,1)S(1)}, bf16[1664,1536]{1,0:T(8,128)(2,1)}, u32[]{:S(2)}) copy-start(bf16[1664,1536]{1,0:T(8,128)(2,1)} %get-tuple-element.73) | copy-start | bytes 15335428
  290.3 6.1 copy-start.8
  290.3 6.1 copy-start.18
  296.4 35.2 %copy-start.38 = (bf16[1664,768]{1,0:T(8,128)(2,1)S(1)}, bf16[1664,768]{1,0:T(8,128)(2,1)}, u32[]{:S(2)}) copy-start(bf16[1664,768]{1,0:T(8,128)(2,1)} %get-tuple-element.52.low_in) | copy-start | bytes 7667716
  340.9 146.9 %collective-permute-start.1 = (bf16[1664,768]{1,0:T(8,128)(2,1)}, bf16[1664,768]{1,0:T(8,128)(2,1)}, u32[]{:S(2)}, u32[]{:S(2)}) collective-permute-start(bf16[1664,768]{1,0:T(8,128)(2,1)} %get-tuple-element.48.own_next), channel_id=1, source_target_pairs={{0,1},{1,0},{2,3},{3,2},{4,5},{5,4},{6,7},{7,6},{8,9},{9,8},{10,11... | collective-permute-start | bytes 7667720 | tf_op jit(solution)/shard_map/ppermute | solution.py:599
  342.6 7.0 %copy-start.31 = (f32[1,1536]{1,0:T(1,128)S(1)}, f32[1,1536]{1,0:T(1,128)}, u32[]{:S(2)}) copy-start(f32[1,1536]{1,0:T(1,128)} %get-tuple-element.62) | copy-start | bytes 18436
  342.6 7.0 %copy-start.32 = (f32[1,1536]{1,0:T(1,128)S(1)}, f32[1,1536]{1,0:T(1,128)}, u32[]{:S(2)}) copy-start(f32[1,1536]{1,0:T(1,128)} %get-tuple-element.61) | copy-start | bytes 18436
  342.6 7.2 %copy-start.29 = (f32[2,768]{1,0:T(2,128)S(1)}, f32[2,768]{1,0:T(2,128)}, u32[]{:S(2)}) copy-start(f32[2,768]{1,0:T(2,128)} %param.15) | copy-start | bytes 18436
  342.6 7.2 %copy-start.33 = (f32[1,768]{1,0:T(1,128)S(1)}, f32[1,768]{1,0:T(1,128)}, u32[]{:S(2)}) copy-start(f32[1,768]{1,0:T(1,128)} %get-tuple-element.60) | copy-start | bytes 9220
  342.6 7.2 %copy-start.34 = (f32[1,768]{1,0:T(1,128)S(1)}, f32[1,768]{1,0:T(1,128)}, u32[]{:S(2)}) copy-start(f32[1,768]{1,0:T(1,128)} %get-tuple-element.59) | copy-start | bytes 9220
  342.6 145.3 %copy-start.1 = (bf16[8,196,768]{2,1,0:T(8,128)(2,1)S(1)}, bf16[8,196,768]{2,1,0:T(8,128)(2,1)}, u32[]{:S(2)}) copy-start(bf16[8,196,768]{2,1,0:T(8,128)(2,1)} %copy-done) | copy-start | bytes 7225348
  342.6 145.3 %copy-start.11 = (f32[1,768]{1,0:T(1,128)S(1)}, f32[1,768]{1,0:T(1,128)}, u32[]{:S(2)}) copy-start(f32[1,768]{1,0:T(1,128)} %get-tuple-element.109.refs_5_.b_first.refs_8_) | copy-start | bytes 9220
  342.6 145.3 %copy-start.16 = (s32[8]{0:T(128)S(1)}, s32[8]{0:T(128)}, u32[]{:S(2)}) copy-start(s32[8]{0:T(128)} %counts.9) | copy-start | bytes 100
  349.2 154.0 %collective-permute-start.3 = (bf16[1664,768]{1,0:T(8,128)(2,1)}, bf16[1664,768]{1,0:T(8,128)(2,1)}, u32[]{:S(2)}, u32[]{:S(2)}) collective-permute-start(bf16[1664,768]{1,0:T(8,128)(2,1)} %get-tuple-element.54.own), channel_id=1, source_target_pairs={{0,1},{1,0},{2,3},{3,2},{4,5},{5,4},{6,7},{7,6},{8,9},{9,8},{10,11... | collective-permute-start | bytes 7667720 | tf_op jit(solution)/shard_map/ppermute | solution.py:599
  487.9 1.7 copy-start.4
  497.6 5.6 copy-start.13
  503.3 2.5 copy-start.2
  609.0 3.0 copy-start.23
  609.0 3.0 copy-start.24
  609.0 3.0 copy-start.25
  609.0 3.0 copy-start.26
  609.0 3.0 copy-start.27
  609.0 3.0 copy-start.28
  612.5 4.0 copy-start.21
  612.5 4.7 copy-start.22
  617.2 4.7 copy-start.19
  617.2 4.7 copy-start.20
Sparse Core Ops, SparseCore 0:
  341.1 267.8 all-reduce.3
